TPU v7x, 32 devices: a whole 2x2x4 slice. The times are simulated.
32 devices in a mesh: dp: 16 (over z, y, x), chan: 2 (over core).
Axes of the slice: x: 2, y: 2, z: 4, core: 2. Of those that a mesh axis runs over, the one named last changes fastest.
Arguments:
- boards: bfloat16 [32, 19, 19, 256], P('dp', None, None, 'chan'), may hold values from -110 to 110
- weights: bfloat16 [6, 9, 256, 256], P(None, None, None, 'chan'), may hold values from -0.125 to 0.125
- gains: float32 [6, 256], P(None, 'chan'), may hold values from 0.5 to 1.5
- shifts: float32 [6, 256], P(None, 'chan'), may hold values from -3 to 3
Outputs:
- features: bfloat16 [32, 19, 19, 256], P('dp', None, None, 'chan')
All inputs are finite; a program needn't handle non-finite values.
Results may differ from a plain program's by a relative error of at most 0.0065.
Values may be sent and summed in bfloat16 or wider, within the bound.
A program may use at most 64 MiB of HBM per device.

v0:
```python
import jax
import jax.numpy as jnp
from jax import lax
from jax.sharding import PartitionSpec as P

EPSILON = 1e-05


def conv_taps(inputs, kernel):
    side = inputs.shape[1]
    padded = jnp.pad(inputs, ((0, 0), (1, 1), (1, 1), (0, 0)))
    total = jnp.zeros((inputs.shape[0] * side * side, kernel.shape[2]), jnp.float32)
    for tap in range(9):
        row, col = divmod(tap, 3)
        window = padded[:, row : row + side, col : col + side, :].reshape(-1, inputs.shape[3])
        total = total + jnp.dot(window, kernel[tap], preferred_element_type=jnp.float32)
    return total.reshape(inputs.shape[0], side, side, kernel.shape[2])


def stats_boards(flat, count):
    sums, squares = lax.psum((jnp.sum(flat, axis=0), jnp.sum(flat * flat, axis=0)), "dp")
    mean = sums / count
    return (mean, squares / count - mean * mean)


def on_device(boards, weights, gains, shifts):
    side = boards.shape[1]
    current = boards
    count = boards.shape[0] * side * side * lax.axis_size("dp")
    skipped = current
    for layer in range(weights.shape[0]):
        if layer % 2 == 0:
            skipped = current
        kernel = weights[layer]
        scale, offset = (gains[layer], shifts[layer])

        def add_channels(total, piece, start, kernel=kernel):
            return conv_taps(piece, kernel)

        empty = jnp.zeros(current.shape[:3] + (kernel.shape[2],), jnp.float32)
        out = add_channels(empty, lax.all_gather(current, "chan", axis=3, tiled=True), jnp.int32(0))
        flat = out.reshape(-1, out.shape[3])
        mean, var = stats_boards(flat, count)
        normed = (out - mean) * lax.rsqrt(var + EPSILON) * scale + offset
        if layer % 2 == 1:
            normed = normed + skipped.astype(jnp.float32)
        current = jnp.maximum(normed, 0.0).astype(jnp.bfloat16)
    return current


def solution(mesh):
    placed = (
        P("dp", None, None, "chan"),
        P(None, None, None, "chan"),
        P(None, "chan"),
        P(None, "chan"),
    )
    return jax.shard_map(
        on_device,
        mesh=mesh,
        in_specs=placed,
        out_specs=P("dp", None, None, "chan"),
        check_vma=False,
    )
```

profile of v0, /device:TPU:0, one launch (start us, length us, event | category | flops | bytes accessed | tf_op | source)
XLA Modules:
  0.0 355.0 jit_solution(226234576069920544)
XLA Ops:
  1.0 2.4 all_gather.18
  3.5 2.6 pad_slice_fusion.40
  18.6 43.4 %all-reduce.11 = (f32[128]{0:T(128)S(1)}, f32[128]{0:T(128)S(1)}) all-reduce(f32[128]{0:T(128)S(1)} %get-tuple-element.16, f32[128]{0:T(128)S(1)} %get-tuple-element.15), channel_id=1, replica_groups=mesh['dp'=16,'chan'=2] {'dp'}, use_global_device_ids=true, to_apply=%region_3.4 | all-reduce | flops 256 | bytes 2048 | tf_op jit(solution)/shard_map/psum | solution.py:21
  62.2 2.1 all_gather.19
  66.6 1.9 reshape.330
  68.5 1.9 reshape.323
  81.6 36.6 %all-reduce.10 = (f32[128]{0:T(128)S(1)}, f32[128]{0:T(128)S(1)}) all-reduce(f32[128]{0:T(128)S(1)} %get-tuple-element.14, f32[128]{0:T(128)S(1)} %get-tuple-element.13), channel_id=1, replica_groups=mesh['dp'=16,'chan'=2] {'dp'}, use_global_device_ids=true, to_apply=%region_7.8 | all-reduce | flops 256 | bytes 2048 | tf_op jit(solution)/shard_map/psum | solution.py:21
  118.3 2.1 all_gather.20
  122.7 1.9 reshape.340
  124.6 1.9 reshape.333
  126.5 1.9 reshape.334
  140.4 38.8 %all-reduce.9 = (f32[128]{0:T(128)S(1)}, f32[128]{0:T(128)S(1)}) all-reduce(f32[128]{0:T(128)S(1)} %get-tuple-element.12, f32[128]{0:T(128)S(1)} %get-tuple-element.11), channel_id=1, replica_groups=mesh['dp'=16,'chan'=2] {'dp'}, use_global_device_ids=true, to_apply=%region_11.12 | all-reduce | flops 256 | bytes 2048 | tf_op jit(solution)/shard_map/psum | solution.py:21
  179.4 2.1 all_gather.21
  185.7 1.9 reshape.343
  187.6 1.9 reshape.344
  201.5 36.6 %all-reduce.8 = (f32[128]{0:T(128)S(1)}, f32[128]{0:T(128)S(1)}) all-reduce(f32[128]{0:T(128)S(1)} %get-tuple-element.10, f32[128]{0:T(128)S(1)} %get-tuple-element.9), channel_id=1, replica_groups=mesh['dp'=16,'chan'=2] {'dp'}, use_global_device_ids=true, to_apply=%region_15.16 | all-reduce | flops 256 | bytes 2048 | tf_op jit(solution)/shard_map/psum | solution.py:21
  238.2 2.1 all_gather.22
  242.6 1.9 reshape.360
  244.5 1.9 reshape.353
  258.4 38.6 %all-reduce.7 = (f32[128]{0:T(128)S(1)}, f32[128]{0:T(128)S(1)}) all-reduce(f32[128]{0:T(128)S(1)} %get-tuple-element.8, f32[128]{0:T(128)S(1)} %get-tuple-element.7), channel_id=1, replica_groups=mesh['dp'=16,'chan'=2] {'dp'}, use_global_device_ids=true, to_apply=%region_19.20 | all-reduce | flops 256 | bytes 2048 | tf_op jit(solution)/shard_map/psum | solution.py:21
  297.2 2.1 all_gather.23
  301.6 1.9 reshape.370
  303.5 1.9 reshape.363
  317.4 36.6 %all-reduce.6 = (f32[128]{0:T(128)S(1)}, f32[128]{0:T(128)S(1)}) all-reduce(f32[128]{0:T(128)S(1)} %get-tuple-element.6, f32[128]{0:T(128)S(1)} %get-tuple-element.5), channel_id=1, replica_groups=mesh['dp'=16,'chan'=2] {'dp'}, use_global_device_ids=true, to_apply=%region_23.24 | all-reduce | flops 256 | bytes 2048 | tf_op jit(solution)/shard_map/psum | solution.py:21
  (155 shorter events, 87.0 us)
Async XLA Ops:
  10.8 6.7 %copy-start.5 = (bf16[722,256]{1,0:T(8,128)(2,1)S(1)}, bf16[722,256]{1,0:T(8,128)(2,1)}, u32[]{:S(2)}) copy-start(bf16[722,256]{1,0:T(8,128)(2,1)} %reshape.320) | copy-start | bytes 1108996
  70.8 5.1 %copy-start = (bf16[722,256]{1,0:T(8,128)(2,1)S(1)}, bf16[722,256]{1,0:T(8,128)(2,1)}, u32[]{:S(2)}) copy-start(bf16[722,256]{1,0:T(8,128)(2,1)} %reshape.326) | copy-start | bytes 1108996
  73.6 6.8 %copy-start.6 = (bf16[722,256]{1,0:T(8,128)(2,1)S(1)}, bf16[722,256]{1,0:T(8,128)(2,1)}, u32[]{:S(2)}) copy-start(bf16[722,256]{1,0:T(8,128)(2,1)} %reshape.330) | copy-start | bytes 1108996
  75.9 42.3 %copy-start.11 = (bf16[2,19,19,128]{3,0,2,1:T(2,128)(2,1)S(1)}, bf16[2,19,19,128]{3,0,2,1:T(2,128)(2,1)}, u32[]{:S(2)}) copy-start(bf16[2,19,19,128]{3,0,2,1:T(2,128)(2,1)} %param.4) | copy-start | bytes 554500
  128.7 6.1 %copy-start.1 = (bf16[722,256]{1,0:T(8,128)(2,1)S(1)}, bf16[722,256]{1,0:T(8,128)(2,1)}, u32[]{:S(2)}) copy-start(bf16[722,256]{1,0:T(8,128)(2,1)} %reshape.336) | copy-start | bytes 1108996
  132.4 6.9 %copy-start.7 = (bf16[722,256]{1,0:T(8,128)(2,1)S(1)}, bf16[722,256]{1,0:T(8,128)(2,1)}, u32[]{:S(2)}) copy-start(bf16[722,256]{1,0:T(8,128)(2,1)} %reshape.340) | copy-start | bytes 1108996
  189.8 6.1 %copy-start.2 = (bf16[722,256]{1,0:T(8,128)(2,1)S(1)}, bf16[722,256]{1,0:T(8,128)(2,1)}, u32[]{:S(2)}) copy-start(bf16[722,256]{1,0:T(8,128)(2,1)} %reshape.346) | copy-start | bytes 1108996
  193.4 6.9 %copy-start.8 = (bf16[722,256]{1,0:T(8,128)(2,1)S(1)}, bf16[722,256]{1,0:T(8,128)(2,1)}, u32[]{:S(2)}) copy-start(bf16[722,256]{1,0:T(8,128)(2,1)} %reshape.350) | copy-start | bytes 1108996
  246.9 5.9 %copy-start.3 = (bf16[722,256]{1,0:T(8,128)(2,1)S(1)}, bf16[722,256]{1,0:T(8,128)(2,1)}, u32[]{:S(2)}) copy-start(bf16[722,256]{1,0:T(8,128)(2,1)} %reshape.356) | copy-start | bytes 1108996
  250.5 6.7 %copy-start.9 = (bf16[722,256]{1,0:T(8,128)(2,1)S(1)}, bf16[722,256]{1,0:T(8,128)(2,1)}, u32[]{:S(2)}) copy-start(bf16[722,256]{1,0:T(8,128)(2,1)} %reshape.360) | copy-start | bytes 1108996
  305.9 5.9 %copy-start.4 = (bf16[722,256]{1,0:T(8,128)(2,1)S(1)}, bf16[722,256]{1,0:T(8,128)(2,1)}, u32[]{:S(2)}) copy-start(bf16[722,256]{1,0:T(8,128)(2,1)} %reshape.366) | copy-start | bytes 1108996
  309.5 6.7 %copy-start.10 = (bf16[722,256]{1,0:T(8,128)(2,1)S(1)}, bf16[722,256]{1,0:T(8,128)(2,1)}, u32[]{:S(2)}) copy-start(bf16[722,256]{1,0:T(8,128)(2,1)} %reshape.370) | copy-start | bytes 1108996
where the time goes:
time: 358 us; the launch traced here: 355 us
  blocking collectives  244 us (68%)
  matrix products  61.8 us (17%)
  local copies, waits for them, and re-layouts  48 us (13%)
    psum x6, blocking collectives, stats_boards(): lax.psum((jnp.sum(flat, axis=0), jnp.sum(flat * flat, axis=0)), 'dp')  231 us
    dot_general x54, matrix products, conv_taps(): jnp.dot(window, kernel[tap], preferred_element_type=jnp.float32)  61.8 us
    reshape x54, local copies, waits for them, and re-layouts, conv_taps(): padded[:, row:row + side, col:col + side, :].reshape(-1, inputs.shape[3])  36 us
    all_gather x6, blocking collectives, on_device(): lax.all_gather(current, 'chan', axis=3, tiled=True)  13.1 us
    slice x14, local copies, waits for them, and re-layouts, conv_taps(): padded[:, row:row + side, col:col + side, :].reshape(-1, inputs.shape[3])  9.93 us

commit v1 on v0

v1 whole, which is shorter than its diff:
```python
import functools

import jax
import jax.numpy as jnp
from jax import lax
from jax.experimental import pallas as pl
from jax.experimental.pallas import tpu as pltpu
from jax.sharding import PartitionSpec as P

EPSILON = 1e-05
MESH = pl.DeviceIdType.MESH
LANES = 128


def round_up(value, step):
    return -(-value // step) * step


def stack_kernel(
    ndp, nch, side, mine, layers, rows, base,
    boards, weights, gains, shifts, out,
    board_own, board_other, wbuf, aff, xf, skip, mask, lhs, zbuf, stats, stage,
    own_sem, x_send, x_recv, w_local, w_send, w_recv, s_send, s_recv, o_send, o_recv,
):
    dp = lax.axis_index("dp")
    me = lax.axis_index("chan")
    other = 1 - me
    partner = (dp, other)
    total = ndp * nch
    flat_me = dp * nch + me
    stride = side + 1
    points = mine * side * side

    def peer(step):
        flat = lax.rem(flat_me + step, total)
        return (lax.div(flat, nch), lax.rem(flat, nch))

    def every_peer(body):
        if total <= 64:
            for step in range(1, total):
                body(step)
        else:
            def one(step, carry):
                body(step)
                return carry
            lax.fori_loop(1, total, one, 0)

    barrier = pltpu.get_barrier_semaphore()
    every_peer(lambda step: pl.semaphore_signal(barrier, inc=1, device_id=peer(step), device_id_type=MESH))

    own = pltpu.make_async_copy(boards.at[pl.ds(me * mine, mine)], board_own, own_sem)
    own.start()

    def weight_local(layer):
        return pltpu.make_async_copy(weights.at[layer], wbuf.at[me, layer], w_local.at[layer])

    def weight_remote(layer, half):
        return pltpu.make_async_remote_copy(
            src_ref=weights.at[layer], dst_ref=wbuf.at[half, layer],
            send_sem=w_send.at[layer], recv_sem=w_recv.at[layer],
            device_id=partner, device_id_type=MESH,
        )

    def swap(index, src, dst):
        return pltpu.make_async_remote_copy(
            src_ref=src, dst_ref=dst, send_sem=x_send.at[index], recv_sem=x_recv.at[index],
            device_id=partner, device_id_type=MESH,
        )

    for layer in range(layers):
        weight_local(layer).start()
    xf[...] = jnp.zeros_like(xf)
    mask[...] = jnp.zeros_like(mask)
    for n in range(mine):
        for i in range(side):
            mask[pl.ds((n * stride + i) * stride, side), :] = jnp.ones((side, LANES), jnp.float32)
    aff[me, 0] = gains[...]
    aff[me, 1] = shifts[...]

    pl.semaphore_wait(barrier, total - 1)
    swaps = [
        swap(0, boards.at[pl.ds(other * mine, mine)], board_other),
        swap(1, gains, aff.at[me, 0]),
        swap(2, shifts, aff.at[me, 1]),
    ]
    swaps[0].start()
    weight_remote(0, me).start()
    swaps[1].start()
    swaps[2].start()
    for layer in range(1, layers):
        weight_remote(layer, me).start()

    def place(half, source):
        for n in range(mine):
            for i in range(side):
                at = base + (n * stride + i) * stride
                xf[half, pl.ds(at, side), :] = source[n, i].astype(jnp.float32)

    own.wait()
    place(me, board_own)
    swaps[0].wait_recv()
    place(other, board_other)
    swaps[1].wait_recv()
    swaps[2].wait_recv()

    def layer_step(layer, carry):
        odd = lax.rem(layer, 2)

        @pl.when(odd == 0)
        def _():
            for half in range(nch):
                skip[half] = xf[half, pl.ds(base, rows), :]

        for tap in range(9):
            a, b = divmod(tap, 3)
            at = base + (a - 1) * stride + (b - 1)
            for half in range(nch):
                column = (tap * nch + half) * LANES
                lhs[:, pl.ds(column, LANES)] = xf[half, pl.ds(at, rows), :].astype(jnp.bfloat16)
        weight_local(layer).wait()
        weight_remote(layer, other).wait_recv()
        kernel = jnp.concatenate([wbuf[half, layer] for half in range(nch)], axis=1)
        zbuf[...] = jnp.dot(lhs[...], kernel, preferred_element_type=jnp.float32)

        centre = (side // 2) * stride + side // 2
        for half in range(nch):
            lanes = pl.ds(half * LANES, LANES)
            middle = zbuf[pl.ds(centre, 1), lanes]
            away = (zbuf[:, lanes] - middle) * mask[...]
            first = jnp.sum(away, axis=0, keepdims=True)
            second = jnp.sum(away * away, axis=0, keepdims=True)
            stats[layer, flat_me, pl.ds(half, 1), :] = middle + first * (1.0 / points)
            stats[layer, flat_me, pl.ds(nch + half, 1), :] = second - first * first * (1.0 / points)

        def send(step):
            pltpu.make_async_remote_copy(
                src_ref=stats.at[layer, flat_me], dst_ref=stats.at[layer, flat_me],
                send_sem=s_send.at[layer], recv_sem=s_recv.at[layer],
                device_id=peer(step), device_id_type=MESH,
            ).start()

        every_peer(send)
        arrived = stats.at[layer, pl.ds(0, total - 1)]
        pltpu.make_async_copy(arrived, arrived, s_recv.at[layer]).wait()

        seen = stats[layer]
        mean = jnp.sum(seen, axis=0)[:nch] * (1.0 / total)
        drift = seen[:, :nch] - mean[None]
        var = (jnp.sum(seen[:, nch:], axis=0) + points * jnp.sum(drift * drift, axis=0)) * (1.0 / (points * total))
        inverse = lax.rsqrt(var + EPSILON)
        keep = odd.astype(jnp.float32)
        for half in range(nch):
            gain = aff[half, 0, pl.ds(layer, 1), :] * inverse[half : half + 1]
            shift = aff[half, 1, pl.ds(layer, 1), :]
            normed = (zbuf[:, pl.ds(half * LANES, LANES)] - mean[half : half + 1]) * gain + shift
            normed = normed + skip[half] * keep
            fresh = jnp.maximum(normed, 0.0) * mask[...]
            xf[half, pl.ds(base, rows), :] = fresh.astype(jnp.bfloat16).astype(jnp.float32)
        return carry

    lax.fori_loop(0, layers, layer_step, 0)

    def collect(half, target, first):
        for n in range(mine):
            for i in range(side):
                at = base + (n * stride + i) * stride
                target[first + n, i] = xf[half, pl.ds(at, side), :].astype(jnp.bfloat16)

    collect(other, stage, 0)
    final = pltpu.make_async_remote_copy(
        src_ref=stage, dst_ref=out.at[pl.ds(me * mine, mine)],
        send_sem=o_send, recv_sem=o_recv, device_id=partner, device_id_type=MESH,
    )
    final.start()
    collect(me, out, me * mine)

    for one in swaps:
        one.wait_send()

    def drain(layer, carry):
        weight_remote(layer, me).wait_send()
        sent = stats.at[layer, pl.ds(0, total - 1)]
        pltpu.make_async_copy(sent, sent, s_send.at[layer]).wait()
        return carry

    lax.fori_loop(0, layers, drain, 0)
    final.wait()


def on_device(ndp, nch, boards, weights, gains, shifts):
    held, side, _, width = boards.shape
    layers = weights.shape[0]
    mine = held // nch
    stride = side + 1
    rows = round_up((mine - 1) * stride * stride + side * stride, 16)
    base = round_up(stride + 1, 8)
    span = round_up(base + rows + stride + 1, 8)
    total = ndp * nch
    depth = 9 * width * nch
    dma = pltpu.SemaphoreType.DMA
    any_space = pl.BlockSpec(memory_space=pl.ANY)
    vmem = pl.BlockSpec(memory_space=pltpu.VMEM)
    return pl.pallas_call(
        functools.partial(stack_kernel, ndp, nch, side, mine, layers, rows, base),
        out_shape=jax.ShapeDtypeStruct(boards.shape, jnp.bfloat16),
        in_specs=[any_space, any_space, vmem, vmem],
        out_specs=vmem,
        scratch_shapes=[
            pltpu.VMEM((mine, side, side, width), jnp.bfloat16),
            pltpu.VMEM((mine, side, side, width), jnp.bfloat16),
            pltpu.VMEM((nch, layers, depth, width), jnp.bfloat16),
            pltpu.VMEM((nch, 2, layers, width), jnp.float32),
            pltpu.VMEM((nch, span, width), jnp.float32),
            pltpu.VMEM((nch, rows, width), jnp.float32),
            pltpu.VMEM((rows, width), jnp.float32),
            pltpu.VMEM((rows, depth), jnp.bfloat16),
            pltpu.VMEM((rows, width * nch), jnp.float32),
            pltpu.VMEM((layers, total, 2 * nch, width), jnp.float32),
            pltpu.VMEM((mine, side, side, width), jnp.bfloat16),
            dma, dma((3,)), dma((3,)),
            dma((layers,)), dma((layers,)), dma((layers,)),
            dma((layers,)), dma((layers,)), dma, dma,
        ],
        compiler_params=pltpu.CompilerParams(
            collective_id=0, has_side_effects=True, vmem_limit_bytes=40 * 1024 * 1024
        ),
        cost_estimate=pl.CostEstimate(
            flops=2 * layers * rows * depth * width * nch,
            bytes_accessed=2 * weights.size + 4 * boards.size,
            transcendentals=0,
        ),
    )(boards, weights.reshape(layers, depth, width), gains, shifts)


def solution(mesh):
    placed = (
        P("dp", None, None, "chan"),
        P(None, None, None, "chan"),
        P(None, "chan"),
        P(None, "chan"),
    )
    return jax.shard_map(
        functools.partial(on_device, mesh.shape["dp"], mesh.shape["chan"]),
        mesh=mesh,
        in_specs=placed,
        out_specs=P("dp", None, None, "chan"),
        check_vma=False,
    )
```

time: 358 us -> 50 us (0.14)
  blocking collectives: 244 us -> 0 us
  matrix products: 61.8 us -> 0 us
  Pallas kernels: 0 us -> 44.6 us
  local copies, waits for them, and re-layouts: 48 us -> 5.14 us
    psum x6 -> x0, blocking collectives: 231 us -> none  [stats_boards(): lax.psum((jnp.sum(flat, axis=0), jnp.sum(flat * flat, axis=0)), 'dp')]
    dot_general x54 -> x0, matrix products: 61.8 us -> none  [conv_taps(): jnp.dot(window, kernel[tap], preferred_element_type=jnp.float32)]
    pallas_call x0 -> x1, Pallas kernels: none -> 44.6 us  [on_device(): pl.pallas_call(functools.partial(stack_kernel, ndp, nch, side, mine, laye...]
    reshape x60 -> x0, local copies, waits for them, and re-layouts: 36.2 us -> none  [the longest x54 36 us: conv_taps(): padded[:, row:row + side, col:col + side, :].reshape(-1, inputs.shape[3])]
    all_gather x6 -> x0, blocking collectives: 13.1 us -> none  [on_device(): lax.all_gather(current, 'chan', axis=3, tiled=True)]
    slice x14 -> x0, local copies, waits for them, and re-layouts: 9.93 us -> none  [conv_taps(): padded[:, row:row + side, col:col + side, :].reshape(-1, inputs.shape[3])]
    unnamed x24 -> x7, local copies, waits for them, and re-layouts: 0.05 us -> 4.32 us
where the time goes in v1:
time: 50 us; the launch traced here: 49.7 us
  Pallas kernels  44.6 us (89%)
  local copies, waits for them, and re-layouts  5.14 us (10%)
    pallas_call x1, Pallas kernels, on_device(): pl.pallas_call(functools.partial(stack_kernel, ndp, nch, side, mine, laye...  44.6 us
    unnamed x7, local copies, waits for them, and re-layouts  4.32 us

profile of v1, /device:TPU:0, one launch (start us, length us, event | category | flops | bytes accessed | tf_op | source)
XLA Modules:
  0.0 49.7 jit_solution(15190654884489416750)
XLA Ops:
  0.0 1.0 %copy.5.boards = bf16[2,19,19,128]{3,2,1,0:T(8,128)(2,1)S(1)} copy(bf16[2,19,19,128]{3,0,2,1:T(2,128)(2,1)} %param.4) | data formatting | bytes 369664 | tf_op args[0]
  1.0 0.0 copy-start
  1.0 2.0 %copy-done = bf16[6,9,256,128]{3,2,1,0:T(8,128)(2,1)S(1)} copy-done((bf16[6,9,256,128]{3,2,1,0:T(8,128)(2,1)S(1)}, bf16[6,9,256,128]{3,2,1,0:T(8,128)(2,1)}, u32[]{:S(2)}) %copy-start) | copy-done | bytes 3538968
  3.0 0.0 copy-start.1
  3.0 0.7 %copy-done.1 = f32[6,128]{1,0:T(8,128)S(1)} copy-done((f32[6,128]{1,0:T(8,128)S(1)}, f32[6,128]{1,0:T(8,128)}, u32[]{:S(2)}) %copy-start.1) | copy-done | bytes 3096
  3.6 0.0 copy-start.2
  3.7 0.7 %copy-done.2 = f32[6,128]{1,0:T(8,128)S(1)} copy-done((f32[6,128]{1,0:T(8,128)S(1)}, f32[6,128]{1,0:T(8,128)}, u32[]{:S(2)}) %copy-start.2) | copy-done | bytes 3096
  4.3 44.6 %shard_map.46 = bf16[2,19,19,128]{3,2,1,0:T(8,128)(2,1)S(1)} custom-call(bf16[2,19,19,128]{3,2,1,0:T(8,128)(2,1)S(1)} %copy.5.boards, bf16[6,2304,128]{2,1,0:T(8,128)(2,1)S(1)} %bitcast.1, f32[6,128]{1,0:T(8,128)S(1)} %copy-done.1, f32[6,128]{1,0:T(8,128)S(1)} %copy-done.2), custom_call_target="tpu_custom_call" | custom-call | flops 2717908992 | bytes 3908608 | tf_op jit(solution)/shard_map/pallas_call | solution.py:203
  48.9 0.8 %copy.6 = bf16[2,19,19,128]{3,0,2,1:T(2,128)(2,1)} copy(bf16[2,19,19,128]{3,2,1,0:T(8,128)(2,1)S(1)} %shard_map.46) | data formatting | bytes 369664 | tf_op jit(solution)/shard_map/pallas_call | solution.py:203
Async XLA Ops:
  1.0 2.0 %copy-start = (bf16[6,9,256,128]{3,2,1,0:T(8,128)(2,1)S(1)}, bf16[6,9,256,128]{3,2,1,0:T(8,128)(2,1)}, u32[]{:S(2)}) copy-start(bf16[6,9,256,128]{3,2,1,0:T(8,128)(2,1)} %param.5) | copy-start | bytes 10616836
  3.0 0.7 %copy-start.1 = (f32[6,128]{1,0:T(8,128)S(1)}, f32[6,128]{1,0:T(8,128)}, u32[]{:S(2)}) copy-start(f32[6,128]{1,0:T(8,128)} %gains.1) | copy-start | bytes 9220
  3.6 0.7 %copy-start.2 = (f32[6,128]{1,0:T(8,128)S(1)}, f32[6,128]{1,0:T(8,128)}, u32[]{:S(2)}) copy-start(f32[6,128]{1,0:T(8,128)} %shifts.1) | copy-start | bytes 9220

commit v2 on v1

--- a/solution.py
+++ b/solution.py
@@ -17,36 +17,35 @@
 
 
 def stack_kernel(
-    ndp, nch, side, mine, layers, rows, base,
+    ndp, nch, inner, side, mine, layers, rows, base,
     boards, weights, gains, shifts, out,
-    board_own, board_other, wbuf, aff, xf, skip, mask, lhs, zbuf, stats, stage,
-    own_sem, x_send, x_recv, w_local, w_send, w_recv, s_send, s_recv, o_send, o_recv,
+    board_own, board_other, wbuf, aff, xf, skip, mask, lhs, zbuf, near, far, stage,
+    own_sem, x_send, x_recv, w_local, w_send, w_recv, n_send, n_recv, f_send, f_recv, o_send, o_recv,
 ):
     dp = lax.axis_index("dp")
     me = lax.axis_index("chan")
     other = 1 - me
     partner = (dp, other)
     total = ndp * nch
-    flat_me = dp * nch + me
     stride = side + 1
     points = mine * side * side
 
-    def peer(step):
-        flat = lax.rem(flat_me + step, total)
-        return (lax.div(flat, nch), lax.rem(flat, nch))
-
-    def every_peer(body):
-        if total <= 64:
-            for step in range(1, total):
-                body(step)
-        else:
-            def one(step, carry):
-                body(step)
-                return carry
-            lax.fori_loop(1, total, one, 0)
+    outer = ndp // inner
+    group = inner * nch
+    plane, spot = lax.div(dp, inner), lax.rem(dp, inner)
+    near_me = spot * nch + me
+
+    def near_peer(step):
+        flat = lax.rem(near_me + step, group)
+        return (plane * inner + lax.div(flat, nch), lax.rem(flat, nch))
+
+    def far_peer(step):
+        return (lax.rem(plane + step, outer) * inner + spot, me)
 
     barrier = pltpu.get_barrier_semaphore()
-    every_peer(lambda step: pl.semaphore_signal(barrier, inc=1, device_id=peer(step), device_id_type=MESH))
+    for count, peer in ((group, near_peer), (outer, far_peer)):
+        for step in range(1, count):
+            pl.semaphore_signal(barrier, inc=1, device_id=peer(step), device_id_type=MESH)
 
     own = pltpu.make_async_copy(boards.at[pl.ds(me * mine, mine)], board_own, own_sem)
     own.start()
@@ -77,7 +76,7 @@
     aff[me, 0] = gains[...]
     aff[me, 1] = shifts[...]
 
-    pl.semaphore_wait(barrier, total - 1)
+    pl.semaphore_wait(barrier, group - 1 + outer - 1)
     swaps = [
         swap(0, boards.at[pl.ds(other * mine, mine)], board_other),
         swap(1, gains, aff.at[me, 0]),
@@ -103,6 +102,25 @@
     swaps[1].wait_recv()
     swaps[2].wait_recv()
 
+    def exchange(slots, layer, place_me, count, peer, send_sem, recv_sem):
+        for step in range(1, count):
+            pltpu.make_async_remote_copy(
+                src_ref=slots.at[layer, place_me], dst_ref=slots.at[layer, place_me],
+                send_sem=send_sem.at[layer], recv_sem=recv_sem.at[layer],
+                device_id=peer(step), device_id_type=MESH,
+            ).start()
+        await_slots(slots, layer, count, recv_sem)
+
+    def await_slots(slots, layer, count, sem):
+        those = slots.at[layer, pl.ds(0, count - 1)]
+        pltpu.make_async_copy(those, those, sem.at[layer]).wait()
+
+    def merge(seen, each):
+        mean = jnp.sum(seen[:, :nch], axis=0) * (1.0 / seen.shape[0])
+        drift = seen[:, :nch] - mean[None]
+        spread = jnp.sum(seen[:, nch:], axis=0) + each * jnp.sum(drift * drift, axis=0)
+        return mean, spread
+
     def layer_step(layer, carry):
         odd = lax.rem(layer, 2)
 
@@ -129,24 +147,16 @@
             away = (zbuf[:, lanes] - middle) * mask[...]
             first = jnp.sum(away, axis=0, keepdims=True)
             second = jnp.sum(away * away, axis=0, keepdims=True)
-            stats[layer, flat_me, pl.ds(half, 1), :] = middle + first * (1.0 / points)
-            stats[layer, flat_me, pl.ds(nch + half, 1), :] = second - first * first * (1.0 / points)
-
-        def send(step):
-            pltpu.make_async_remote_copy(
-                src_ref=stats.at[layer, flat_me], dst_ref=stats.at[layer, flat_me],
-                send_sem=s_send.at[layer], recv_sem=s_recv.at[layer],
-                device_id=peer(step), device_id_type=MESH,
-            ).start()
-
-        every_peer(send)
-        arrived = stats.at[layer, pl.ds(0, total - 1)]
-        pltpu.make_async_copy(arrived, arrived, s_recv.at[layer]).wait()
-
-        seen = stats[layer]
-        mean = jnp.sum(seen, axis=0)[:nch] * (1.0 / total)
-        drift = seen[:, :nch] - mean[None]
-        var = (jnp.sum(seen[:, nch:], axis=0) + points * jnp.sum(drift * drift, axis=0)) * (1.0 / (points * total))
+            near[layer, near_me, pl.ds(half, 1), :] = middle + first * (1.0 / points)
+            near[layer, near_me, pl.ds(nch + half, 1), :] = second - first * first * (1.0 / points)
+
+        exchange(near, layer, near_me, group, near_peer, n_send, n_recv)
+        mean, spread = merge(near[layer], points)
+        far[layer, plane, pl.ds(0, nch), :] = mean
+        far[layer, plane, pl.ds(nch, nch), :] = spread
+        exchange(far, layer, plane, outer, far_peer, f_send, f_recv)
+        mean, spread = merge(far[layer], points * group)
+        var = spread * (1.0 / (points * total))
         inverse = lax.rsqrt(var + EPSILON)
         keep = odd.astype(jnp.float32)
         for half in range(nch):
@@ -179,8 +189,8 @@
 
     def drain(layer, carry):
         weight_remote(layer, me).wait_send()
-        sent = stats.at[layer, pl.ds(0, total - 1)]
-        pltpu.make_async_copy(sent, sent, s_send.at[layer]).wait()
+        await_slots(near, layer, group, n_send)
+        await_slots(far, layer, outer, f_send)
         return carry
 
     lax.fori_loop(0, layers, drain, 0)
@@ -195,15 +205,15 @@
     rows = round_up((mine - 1) * stride * stride + side * stride, 16)
     base = round_up(stride + 1, 8)
     span = round_up(base + rows + stride + 1, 8)
-    total = ndp * nch
+    inner = 1 << ((ndp.bit_length() - 1) // 2)
     depth = 9 * width * nch
     dma = pltpu.SemaphoreType.DMA
-    any_space = pl.BlockSpec(memory_space=pl.ANY)
+    in_hbm = pl.BlockSpec(memory_space=pltpu.HBM)
     vmem = pl.BlockSpec(memory_space=pltpu.VMEM)
     return pl.pallas_call(
-        functools.partial(stack_kernel, ndp, nch, side, mine, layers, rows, base),
+        functools.partial(stack_kernel, ndp, nch, inner, side, mine, layers, rows, base),
         out_shape=jax.ShapeDtypeStruct(boards.shape, jnp.bfloat16),
-        in_specs=[any_space, any_space, vmem, vmem],
+        in_specs=[in_hbm, in_hbm, vmem, vmem],
         out_specs=vmem,
         scratch_shapes=[
             pltpu.VMEM((mine, side, side, width), jnp.bfloat16),
@@ -215,14 +225,15 @@
             pltpu.VMEM((rows, width), jnp.float32),
             pltpu.VMEM((rows, depth), jnp.bfloat16),
             pltpu.VMEM((rows, width * nch), jnp.float32),
-            pltpu.VMEM((layers, total, 2 * nch, width), jnp.float32),
+            pltpu.VMEM((layers, inner * nch, 2 * nch, width), jnp.float32),
+            pltpu.VMEM((layers, ndp // inner, 2 * nch, width), jnp.float32),
             pltpu.VMEM((mine, side, side, width), jnp.bfloat16),
             dma, dma((3,)), dma((3,)),
             dma((layers,)), dma((layers,)), dma((layers,)),
-            dma((layers,)), dma((layers,)), dma, dma,
+            dma((layers,)), dma((layers,)), dma((layers,)), dma((layers,)), dma, dma,
         ],
         compiler_params=pltpu.CompilerParams(
-            collective_id=0, has_side_effects=True, vmem_limit_bytes=40 * 1024 * 1024
+            collective_id=0, has_side_effects=True, vmem_limit_bytes=62 * 1024 * 1024
         ),
         cost_estimate=pl.CostEstimate(
             flops=2 * layers * rows * depth * width * nch,

time: 50 us -> 58.7 us (1.17)
  Pallas kernels: 44.6 us -> 55.1 us
  local copies, waits for them, and re-layouts: 5.14 us -> 3.39 us
    pallas_call x1, Pallas kernels: 44.6 us -> 55.1 us  [on_device(): pl.pallas_call(functools.partial(stack_kernel, ndp, nch, inner, side, min...]
    unnamed x7 -> x1, local copies, waits for them, and re-layouts: 4.32 us -> 1.63 us
    pallas_call x1, local copies, waits for them, and re-layouts: 0.82 us -> 1.76 us  [on_device(): pl.pallas_call(functools.partial(stack_kernel, ndp, nch, inner, side, min...]
where the time goes in v2:
time: 58.7 us; the launch traced here: 58.5 us
  Pallas kernels  55.1 us (94%)
  local copies, waits for them, and re-layouts  3.39 us (6%)
    pallas_call x1, Pallas kernels, on_device(): pl.pallas_call(functools.partial(stack_kernel, ndp, nch, inner, side, min...  55.1 us
    pallas_call x1, local copies, waits for them, and re-layouts, on_device(): pl.pallas_call(functools.partial(stack_kernel, ndp, nch, inner, side, min...  1.76 us
    unnamed x1, local copies, waits for them, and re-layouts  1.63 us

profile of v2, /device:TPU:0, one launch (start us, length us, event | category | flops | bytes accessed | tf_op | source)
XLA Modules:
  0.0 58.5 jit_solution(3073150950784622729)
XLA Ops:
  0.0 1.6 %copy.5.boards = bf16[2,19,19,128]{3,2,1,0:T(8,128)(2,1)} copy(bf16[2,19,19,128]{3,0,2,1:T(2,128)(2,1)} %param.4) | data formatting | bytes 369664 | tf_op args[0]
  1.6 55.1 %shard_map.46 = bf16[2,19,19,128]{3,2,1,0:T(8,128)(2,1)} custom-call(bf16[2,19,19,128]{3,2,1,0:T(8,128)(2,1)} %copy.5.boards, bf16[6,2304,128]{2,1,0:T(8,128)(2,1)} %bitcast.1, f32[6,128]{1,0:T(8,128)} %gains.1, f32[6,128]{1,0:T(8,128)} %shifts.1), custom_call_target="tpu_custom_call" | custom-call | flops 2717908992 | bytes 3908608 | tf_op jit(solution)/shard_map/pallas_call | solution.py:213
  56.8 1.8 %copy.6 = bf16[2,19,19,128]{3,0,2,1:T(2,128)(2,1)} copy(bf16[2,19,19,128]{3,2,1,0:T(8,128)(2,1)} %shard_map.46) | data formatting | bytes 369664 | tf_op jit(solution)/shard_map/pallas_call | solution.py:213

commit v3 on v1

--- a/solution.py
+++ b/solution.py
@@ -10,6 +10,7 @@
 EPSILON = 1e-05
 MESH = pl.DeviceIdType.MESH
 LANES = 128
+VMEM_LIMIT = 57 * 1024 * 1024
 
 
 def round_up(value, step):
@@ -20,7 +21,7 @@
     ndp, nch, side, mine, layers, rows, base,
     boards, weights, gains, shifts, out,
     board_own, board_other, wbuf, aff, xf, skip, mask, lhs, zbuf, stats, stage,
-    own_sem, x_send, x_recv, w_local, w_send, w_recv, s_send, s_recv, o_send, o_recv,
+    own_sem, a_local, x_send, x_recv, w_local, w_send, w_recv, s_send, s_recv, o_send, o_recv,
 ):
     dp = lax.axis_index("dp")
     me = lax.axis_index("chan")
@@ -50,6 +51,12 @@
 
     own = pltpu.make_async_copy(boards.at[pl.ds(me * mine, mine)], board_own, own_sem)
     own.start()
+    affine = [
+        pltpu.make_async_copy(gains, aff.at[me, 0], a_local.at[0]),
+        pltpu.make_async_copy(shifts, aff.at[me, 1], a_local.at[1]),
+    ]
+    for one in affine:
+        one.start()
 
     def weight_local(layer):
         return pltpu.make_async_copy(weights.at[layer], wbuf.at[me, layer], w_local.at[layer])
@@ -74,8 +81,6 @@
     for n in range(mine):
         for i in range(side):
             mask[pl.ds((n * stride + i) * stride, side), :] = jnp.ones((side, LANES), jnp.float32)
-    aff[me, 0] = gains[...]
-    aff[me, 1] = shifts[...]
 
     pl.semaphore_wait(barrier, total - 1)
     swaps = [
@@ -87,8 +92,6 @@
     weight_remote(0, me).start()
     swaps[1].start()
     swaps[2].start()
-    for layer in range(1, layers):
-        weight_remote(layer, me).start()
 
     def place(half, source):
         for n in range(mine):
@@ -102,9 +105,15 @@
     place(other, board_other)
     swaps[1].wait_recv()
     swaps[2].wait_recv()
+    for one in affine:
+        one.wait()
 
     def layer_step(layer, carry):
         odd = lax.rem(layer, 2)
+
+        @pl.when(layer + 1 < layers)
+        def _():
+            weight_remote(layer + 1, me).start()
 
         @pl.when(odd == 0)
         def _():
@@ -198,12 +207,12 @@
     total = ndp * nch
     depth = 9 * width * nch
     dma = pltpu.SemaphoreType.DMA
-    any_space = pl.BlockSpec(memory_space=pl.ANY)
+    in_hbm = pl.BlockSpec(memory_space=pltpu.HBM)
     vmem = pl.BlockSpec(memory_space=pltpu.VMEM)
     return pl.pallas_call(
         functools.partial(stack_kernel, ndp, nch, side, mine, layers, rows, base),
         out_shape=jax.ShapeDtypeStruct(boards.shape, jnp.bfloat16),
-        in_specs=[any_space, any_space, vmem, vmem],
+        in_specs=[in_hbm] * 4,
         out_specs=vmem,
         scratch_shapes=[
             pltpu.VMEM((mine, side, side, width), jnp.bfloat16),
@@ -217,12 +226,12 @@
             pltpu.VMEM((rows, width * nch), jnp.float32),
             pltpu.VMEM((layers, total, 2 * nch, width), jnp.float32),
             pltpu.VMEM((mine, side, side, width), jnp.bfloat16),
-            dma, dma((3,)), dma((3,)),
+            dma, dma((2,)), dma((3,)), dma((3,)),
             dma((layers,)), dma((layers,)), dma((layers,)),
             dma((layers,)), dma((layers,)), dma, dma,
         ],
         compiler_params=pltpu.CompilerParams(
-            collective_id=0, has_side_effects=True, vmem_limit_bytes=40 * 1024 * 1024
+            collective_id=0, has_side_effects=True, vmem_limit_bytes=VMEM_LIMIT
         ),
         cost_estimate=pl.CostEstimate(
             flops=2 * layers * rows * depth * width * nch,

time: 50 us -> 49.1 us (0.982)
  local copies, waits for them, and re-layouts: 5.14 us -> 3.39 us
  Pallas kernels: 44.6 us -> 45.5 us
    unnamed x7 -> x1, local copies, waits for them, and re-layouts: 4.32 us -> 1.63 us
    pallas_call x1, Pallas kernels: 44.6 us -> 45.5 us  [on_device(): pl.pallas_call(functools.partial(stack_kernel, ndp, nch, side, mine, laye...]
    pallas_call x1, local copies, waits for them, and re-layouts: 0.82 us -> 1.76 us  [on_device(): pl.pallas_call(functools.partial(stack_kernel, ndp, nch, side, mine, laye...]
where the time goes in v3:
time: 49.1 us; the launch traced here: 48.9 us
  Pallas kernels  45.5 us (93%)
  local copies, waits for them, and re-layouts  3.39 us (7%)
    pallas_call x1, Pallas kernels, on_device(): pl.pallas_call(functools.partial(stack_kernel, ndp, nch, side, mine, laye...  45.5 us
    pallas_call x1, local copies, waits for them, and re-layouts, on_device(): pl.pallas_call(functools.partial(stack_kernel, ndp, nch, side, mine, laye...  1.76 us
    unnamed x1, local copies, waits for them, and re-layouts  1.63 us

profile of v3, /device:TPU:0, one launch (start us, length us, event | category | flops | bytes accessed | tf_op | source)
XLA Modules:
  0.0 48.9 jit_solution(2822257213857755200)
XLA Ops:
  0.0 1.6 %copy.5.boards = bf16[2,19,19,128]{3,2,1,0:T(8,128)(2,1)} copy(bf16[2,19,19,128]{3,0,2,1:T(2,128)(2,1)} %param.4) | data formatting | bytes 369664 | tf_op args[0]
  1.6 45.5 %shard_map.46 = bf16[2,19,19,128]{3,2,1,0:T(8,128)(2,1)} custom-call(bf16[2,19,19,128]{3,2,1,0:T(8,128)(2,1)} %copy.5.boards, bf16[6,2304,128]{2,1,0:T(8,128)(2,1)} %bitcast.1, f32[6,128]{1,0:T(8,128)} %gains.1, f32[6,128]{1,0:T(8,128)} %shifts.1), custom_call_target="tpu_custom_call" | custom-call | flops 2717908992 | bytes 3908608 | tf_op jit(solution)/shard_map/pallas_call | solution.py:212
  47.2 1.8 %copy.6 = bf16[2,19,19,128]{3,0,2,1:T(2,128)(2,1)} copy(bf16[2,19,19,128]{3,2,1,0:T(8,128)(2,1)} %shard_map.46) | data formatting | bytes 369664 | tf_op jit(solution)/shard_map/pallas_call | solution.py:212

commit v4 on v3

--- a/solution.py
+++ b/solution.py
@@ -10,7 +10,7 @@
 EPSILON = 1e-05
 MESH = pl.DeviceIdType.MESH
 LANES = 128
-VMEM_LIMIT = 57 * 1024 * 1024
+VMEM_LIMIT = 52 * 1024 * 1024
 
 
 def round_up(value, step):
@@ -19,7 +19,7 @@
 
 def stack_kernel(
     ndp, nch, side, mine, layers, rows, base,
-    boards, weights, gains, shifts, out,
+    boards, weights, affine, out,
     board_own, board_other, wbuf, aff, xf, skip, mask, lhs, zbuf, stats, stage,
     own_sem, a_local, x_send, x_recv, w_local, w_send, w_recv, s_send, s_recv, o_send, o_recv,
 ):
@@ -32,31 +32,33 @@
     stride = side + 1
     points = mine * side * side
 
-    def peer(step):
-        flat = lax.rem(flat_me + step, total)
-        return (lax.div(flat, nch), lax.rem(flat, nch))
+    def flip(index, step):
+        bit = 1
+        while bit <= step:
+            if step & bit:
+                index = index + bit - 2 * bit * lax.rem(lax.div(index, bit), 2)
+            bit *= 2
+        return index
 
     def every_peer(body):
-        if total <= 64:
-            for step in range(1, total):
-                body(step)
+        if total <= 64 and total & (total - 1) == 0:
+            for step in range(total - 1, 0, -1):
+                flat = flip(flat_me, step)
+                body((lax.div(flat, nch), lax.rem(flat, nch)))
         else:
             def one(step, carry):
-                body(step)
+                flat = lax.rem(flat_me + step, total)
+                body((lax.div(flat, nch), lax.rem(flat, nch)))
                 return carry
             lax.fori_loop(1, total, one, 0)
 
     barrier = pltpu.get_barrier_semaphore()
-    every_peer(lambda step: pl.semaphore_signal(barrier, inc=1, device_id=peer(step), device_id_type=MESH))
+    every_peer(lambda peer: pl.semaphore_signal(barrier, inc=1, device_id=peer, device_id_type=MESH))
 
     own = pltpu.make_async_copy(boards.at[pl.ds(me * mine, mine)], board_own, own_sem)
     own.start()
-    affine = [
-        pltpu.make_async_copy(gains, aff.at[me, 0], a_local.at[0]),
-        pltpu.make_async_copy(shifts, aff.at[me, 1], a_local.at[1]),
-    ]
-    for one in affine:
-        one.start()
+    affine_own = pltpu.make_async_copy(affine, aff.at[me], a_local)
+    affine_own.start()
 
     def weight_local(layer):
         return pltpu.make_async_copy(weights.at[layer], wbuf.at[me, layer], w_local.at[layer])
@@ -85,13 +87,11 @@
     pl.semaphore_wait(barrier, total - 1)
     swaps = [
         swap(0, boards.at[pl.ds(other * mine, mine)], board_other),
-        swap(1, gains, aff.at[me, 0]),
-        swap(2, shifts, aff.at[me, 1]),
+        swap(1, affine, aff.at[me]),
     ]
     swaps[0].start()
     weight_remote(0, me).start()
     swaps[1].start()
-    swaps[2].start()
 
     def place(half, source):
         for n in range(mine):
@@ -104,9 +104,7 @@
     swaps[0].wait_recv()
     place(other, board_other)
     swaps[1].wait_recv()
-    swaps[2].wait_recv()
-    for one in affine:
-        one.wait()
+    affine_own.wait()
 
     def layer_step(layer, carry):
         odd = lax.rem(layer, 2)
@@ -114,11 +112,6 @@
         @pl.when(layer + 1 < layers)
         def _():
             weight_remote(layer + 1, me).start()
-
-        @pl.when(odd == 0)
-        def _():
-            for half in range(nch):
-                skip[half] = xf[half, pl.ds(base, rows), :]
 
         for tap in range(9):
             a, b = divmod(tap, 3)
@@ -141,14 +134,20 @@
             stats[layer, flat_me, pl.ds(half, 1), :] = middle + first * (1.0 / points)
             stats[layer, flat_me, pl.ds(nch + half, 1), :] = second - first * first * (1.0 / points)
 
-        def send(step):
+        def send(peer):
             pltpu.make_async_remote_copy(
                 src_ref=stats.at[layer, flat_me], dst_ref=stats.at[layer, flat_me],
                 send_sem=s_send.at[layer], recv_sem=s_recv.at[layer],
-                device_id=peer(step), device_id_type=MESH,
+                device_id=peer, device_id_type=MESH,
             ).start()
 
         every_peer(send)
+
+        @pl.when(odd == 0)
+        def _():
+            for half in range(nch):
+                skip[half] = xf[half, pl.ds(base, rows), :]
+
         arrived = stats.at[layer, pl.ds(0, total - 1)]
         pltpu.make_async_copy(arrived, arrived, s_recv.at[layer]).wait()
 
@@ -212,7 +211,7 @@
     return pl.pallas_call(
         functools.partial(stack_kernel, ndp, nch, side, mine, layers, rows, base),
         out_shape=jax.ShapeDtypeStruct(boards.shape, jnp.bfloat16),
-        in_specs=[in_hbm] * 4,
+        in_specs=[in_hbm] * 3,
         out_specs=vmem,
         scratch_shapes=[
             pltpu.VMEM((mine, side, side, width), jnp.bfloat16),
@@ -226,7 +225,7 @@
             pltpu.VMEM((rows, width * nch), jnp.float32),
             pltpu.VMEM((layers, total, 2 * nch, width), jnp.float32),
             pltpu.VMEM((mine, side, side, width), jnp.bfloat16),
-            dma, dma((2,)), dma((3,)), dma((3,)),
+            dma, dma, dma((2,)), dma((2,)),
             dma((layers,)), dma((layers,)), dma((layers,)),
             dma((layers,)), dma((layers,)), dma, dma,
         ],
@@ -238,7 +237,7 @@
             bytes_accessed=2 * weights.size + 4 * boards.size,
             transcendentals=0,
         ),
-    )(boards, weights.reshape(layers, depth, width), gains, shifts)
+    )(boards, weights.reshape(layers, depth, width), jnp.stack([gains, shifts]))
 
 
 def solution(mesh):

time: 49.1 us -> 45.7 us (0.931)
  Pallas kernels: 45.5 us -> 43 us
  local copies, waits for them, and re-layouts: 3.39 us -> 1.77 us
  other arithmetic: 0 us -> 0.71 us
    pallas_call x1, Pallas kernels: 45.5 us -> 43 us  [on_device(): pl.pallas_call(functools.partial(stack_kernel, ndp, nch, side, mine, laye...]
    pallas_call x1, local copies, waits for them, and re-layouts: 1.76 us -> 0.82 us  [on_device(): pl.pallas_call(functools.partial(stack_kernel, ndp, nch, side, mine, laye...]
    another operation x0 -> x1, other arithmetic: none -> 0.71 us  [on_device(): jnp.stack([gains, shifts])]
    unnamed x1, local copies, waits for them, and re-layouts: 1.63 us -> 0.95 us
where the time goes in v4:
time: 45.7 us; the launch traced here: 45.5 us
  Pallas kernels  43 us (94%)
  local copies, waits for them, and re-layouts  1.77 us (4%)
  other arithmetic  0.71 us (2%)
    pallas_call x1, Pallas kernels, on_device(): pl.pallas_call(functools.partial(stack_kernel, ndp, nch, side, mine, laye...  43 us
    unnamed x1, local copies, waits for them, and re-layouts  0.95 us

profile of v4, /device:TPU:0, one launch (start us, length us, event | category | flops | bytes accessed | tf_op | source)
XLA Modules:
  0.0 45.5 jit_solution(11874759340464741537)
XLA Ops:
  0.0 0.7 %pad_maximum_fusion.affine = f32[2,6,128]{2,1,0:T(8,128)S(1)} fusion(f32[1,6,128]{2,1,0:T(8,128)} %bitcast.3, f32[1,6,128]{2,1,0:T(8,128)} %bitcast.4), kind=kLoop, calls=%fused_computation | loop fusion | flops 1536 | bytes 12288 | tf_op jit(solution)/shard_map/stack | solution.py:240
  0.7 1.0 %copy.5.boards = bf16[2,19,19,128]{3,2,1,0:T(8,128)(2,1)S(1)} copy(bf16[2,19,19,128]{3,0,2,1:T(2,128)(2,1)} %param.4) | data formatting | bytes 369664 | tf_op args[0]
  1.7 43.0 %shard_map.46 = bf16[2,19,19,128]{3,2,1,0:T(8,128)(2,1)S(1)} custom-call(bf16[2,19,19,128]{3,2,1,0:T(8,128)(2,1)S(1)} %copy.5.boards, bf16[6,2304,128]{2,1,0:T(8,128)(2,1)} %bitcast.5, f32[2,6,128]{2,1,0:T(8,128)S(1)} %pad_maximum_fusion.affine), custom_call_target="tpu_custom_call" | custom-call | flops 2717908992 | bytes 3908608 | tf_op jit(solution)/shard_map/pallas_call | solution.py:211
  44.7 0.8 %copy.6 = bf16[2,19,19,128]{3,0,2,1:T(2,128)(2,1)} copy(bf16[2,19,19,128]{3,2,1,0:T(8,128)(2,1)S(1)} %shard_map.46) | data formatting | bytes 369664 | tf_op jit(solution)/shard_map/pallas_call | solution.py:211

commit v5 on v4

--- a/solution.py
+++ b/solution.py
@@ -18,9 +18,9 @@
 
 
 def stack_kernel(
-    ndp, nch, side, mine, layers, rows, base,
+    ndp, nch, side, mine, layers, rows, base, reach,
     boards, weights, affine, out,
-    board_own, board_other, wbuf, aff, xf, skip, mask, lhs, zbuf, stats, stage,
+    board_own, board_other, wbuf, aff, xf, skip, mask, shifted, zbuf, stats, stage,
     own_sem, a_local, x_send, x_recv, w_local, w_send, w_recv, s_send, s_recv, o_send, o_recv,
 ):
     dp = lax.axis_index("dp")
@@ -113,16 +113,18 @@
         def _():
             weight_remote(layer + 1, me).start()
 
-        for tap in range(9):
-            a, b = divmod(tap, 3)
-            at = base + (a - 1) * stride + (b - 1)
+        for b in range(3):
             for half in range(nch):
-                column = (tap * nch + half) * LANES
-                lhs[:, pl.ds(column, LANES)] = xf[half, pl.ds(at, rows), :].astype(jnp.bfloat16)
+                shifted[b, half] = xf[half, pl.ds(base - stride + b - 1, reach), :].astype(jnp.bfloat16)
+        taps = [
+            shifted[tap % 3, half, pl.ds((tap // 3) * stride, rows), :]
+            for tap in range(9) for half in range(nch)
+        ]
+        sample = jnp.concatenate(taps, axis=1)
         weight_local(layer).wait()
         weight_remote(layer, other).wait_recv()
         kernel = jnp.concatenate([wbuf[half, layer] for half in range(nch)], axis=1)
-        zbuf[...] = jnp.dot(lhs[...], kernel, preferred_element_type=jnp.float32)
+        zbuf[...] = jnp.dot(sample, kernel, preferred_element_type=jnp.float32)
 
         centre = (side // 2) * stride + side // 2
         for half in range(nch):
@@ -202,14 +204,15 @@
     stride = side + 1
     rows = round_up((mine - 1) * stride * stride + side * stride, 16)
     base = round_up(stride + 1, 8)
-    span = round_up(base + rows + stride + 1, 8)
+    reach = round_up(rows + 2 * stride, 16)
+    span = round_up(base - stride + 1 + reach, 8)
     total = ndp * nch
     depth = 9 * width * nch
     dma = pltpu.SemaphoreType.DMA
     in_hbm = pl.BlockSpec(memory_space=pltpu.HBM)
     vmem = pl.BlockSpec(memory_space=pltpu.VMEM)
     return pl.pallas_call(
-        functools.partial(stack_kernel, ndp, nch, side, mine, layers, rows, base),
+        functools.partial(stack_kernel, ndp, nch, side, mine, layers, rows, base, reach),
         out_shape=jax.ShapeDtypeStruct(boards.shape, jnp.bfloat16),
         in_specs=[in_hbm] * 3,
         out_specs=vmem,
@@ -221,7 +224,7 @@
             pltpu.VMEM((nch, span, width), jnp.float32),
             pltpu.VMEM((nch, rows, width), jnp.float32),
             pltpu.VMEM((rows, width), jnp.float32),
-            pltpu.VMEM((rows, depth), jnp.bfloat16),
+            pltpu.VMEM((3, nch, reach, width), jnp.bfloat16),
             pltpu.VMEM((rows, width * nch), jnp.float32),
             pltpu.VMEM((layers, total, 2 * nch, width), jnp.float32),
             pltpu.VMEM((mine, side, side, width), jnp.bfloat16),

time: 45.7 us -> 45.9 us (level)
  no operation moved by 1% of the time
where the time goes in v5:
time: 45.9 us; the launch traced here: 45.7 us
  Pallas kernels  43.2 us (94%)
  local copies, waits for them, and re-layouts  1.77 us (4%)
  other arithmetic  0.71 us (2%)
    pallas_call x1, Pallas kernels, on_device(): pl.pallas_call(functools.partial(stack_kernel, ndp, nch, side, mine, laye...  43.2 us
    unnamed x1, local copies, waits for them, and re-layouts  0.95 us

profile of v5, /device:TPU:0, one launch (start us, length us, event | category | flops | bytes accessed | tf_op | source)
XLA Modules:
  0.0 45.7 jit_solution(15964251622017356344)
XLA Ops:
  0.0 0.7 %pad_maximum_fusion.affine = f32[2,6,128]{2,1,0:T(8,128)S(1)} fusion(f32[1,6,128]{2,1,0:T(8,128)} %bitcast.3, f32[1,6,128]{2,1,0:T(8,128)} %bitcast.4), kind=kLoop, calls=%fused_computation | loop fusion | flops 1536 | bytes 12288 | tf_op jit(solution)/shard_map/stack | solution.py:243
  0.7 1.0 %copy.5.boards = bf16[2,19,19,128]{3,2,1,0:T(8,128)(2,1)S(1)} copy(bf16[2,19,19,128]{3,0,2,1:T(2,128)(2,1)} %param.4) | data formatting | bytes 369664 | tf_op args[0]
  1.7 43.2 %shard_map.46 = bf16[2,19,19,128]{3,2,1,0:T(8,128)(2,1)S(1)} custom-call(bf16[2,19,19,128]{3,2,1,0:T(8,128)(2,1)S(1)} %copy.5.boards, bf16[6,2304,128]{2,1,0:T(8,128)(2,1)} %bitcast.5, f32[2,6,128]{2,1,0:T(8,128)S(1)} %pad_maximum_fusion.affine), custom_call_target="tpu_custom_call" | custom-call | flops 2717908992 | bytes 3908608 | tf_op jit(solution)/shard_map/pallas_call | solution.py:214
  44.8 0.8 %copy.6 = bf16[2,19,19,128]{3,0,2,1:T(2,128)(2,1)} copy(bf16[2,19,19,128]{3,2,1,0:T(8,128)(2,1)S(1)} %shard_map.46) | data formatting | bytes 369664 | tf_op jit(solution)/shard_map/pallas_call | solution.py:214

commit v6 on v4

--- a/solution.py
+++ b/solution.py
@@ -20,7 +20,7 @@
 def stack_kernel(
     ndp, nch, side, mine, layers, rows, base,
     boards, weights, affine, out,
-    board_own, board_other, wbuf, aff, xf, skip, mask, lhs, zbuf, stats, stage,
+    raw, board_send, board_other, wbuf, aff, xf, skip, mask, lhs, zbuf, stats, stage,
     own_sem, a_local, x_send, x_recv, w_local, w_send, w_recv, s_send, s_recv, o_send, o_recv,
 ):
     dp = lax.axis_index("dp")
@@ -55,7 +55,7 @@
     barrier = pltpu.get_barrier_semaphore()
     every_peer(lambda peer: pl.semaphore_signal(barrier, inc=1, device_id=peer, device_id_type=MESH))
 
-    own = pltpu.make_async_copy(boards.at[pl.ds(me * mine, mine)], board_own, own_sem)
+    own = pltpu.make_async_copy(boards, raw, own_sem)
     own.start()
     affine_own = pltpu.make_async_copy(affine, aff.at[me], a_local)
     affine_own.start()
@@ -84,9 +84,20 @@
         for i in range(side):
             mask[pl.ds((n * stride + i) * stride, side), :] = jnp.ones((side, LANES), jnp.float32)
 
+    own.wait()
+    for i in range(side):
+        line = raw[i].astype(jnp.float32)
+        for n in range(mine):
+            at = base + (n * stride + i) * stride
+            planes = [line[:, half * mine + n, :] for half in range(nch)]
+            kept = jnp.where(me == 0, planes[0], planes[1])
+            given = jnp.where(me == 0, planes[1], planes[0])
+            xf[me, pl.ds(at, side), :] = kept
+            board_send[n, i] = given.astype(jnp.bfloat16)
+
     pl.semaphore_wait(barrier, total - 1)
     swaps = [
-        swap(0, boards.at[pl.ds(other * mine, mine)], board_other),
+        swap(0, board_send, board_other),
         swap(1, affine, aff.at[me]),
     ]
     swaps[0].start()
@@ -99,8 +110,6 @@
                 at = base + (n * stride + i) * stride
                 xf[half, pl.ds(at, side), :] = source[n, i].astype(jnp.float32)
 
-    own.wait()
-    place(me, board_own)
     swaps[0].wait_recv()
     place(other, board_other)
     swaps[1].wait_recv()
@@ -152,9 +161,12 @@
         pltpu.make_async_copy(arrived, arrived, s_recv.at[layer]).wait()
 
         seen = stats[layer]
-        mean = jnp.sum(seen, axis=0)[:nch] * (1.0 / total)
-        drift = seen[:, :nch] - mean[None]
-        var = (jnp.sum(seen[:, nch:], axis=0) + points * jnp.sum(drift * drift, axis=0)) * (1.0 / (points * total))
+        mine_mean = stats[layer, flat_me, pl.ds(0, nch), :]
+        drift = seen[:, :nch] - mine_mean[None]
+        shifted = jnp.sum(drift, axis=0)
+        spread = jnp.sum(points * drift * drift + seen[:, nch:], axis=0)
+        mean = mine_mean + shifted * (1.0 / total)
+        var = (spread - shifted * shifted * (points / total)) * (1.0 / (points * total))
         inverse = lax.rsqrt(var + EPSILON)
         keep = odd.astype(jnp.float32)
         for half in range(nch):
@@ -214,6 +226,7 @@
         in_specs=[in_hbm] * 3,
         out_specs=vmem,
         scratch_shapes=[
+            pltpu.VMEM((side, side, held, width), jnp.bfloat16),
             pltpu.VMEM((mine, side, side, width), jnp.bfloat16),
             pltpu.VMEM((mine, side, side, width), jnp.bfloat16),
             pltpu.VMEM((nch, layers, depth, width), jnp.bfloat16),
@@ -237,7 +250,7 @@
             bytes_accessed=2 * weights.size + 4 * boards.size,
             transcendentals=0,
         ),
-    )(boards, weights.reshape(layers, depth, width), jnp.stack([gains, shifts]))
+    )(boards.transpose(1, 2, 0, 3), weights.reshape(layers, depth, width), jnp.stack([gains, shifts]))
 
 
 def solution(mesh):

time: 45.7 us -> 45.5 us (level)
    unnamed x1 -> x2, local copies, waits for them, and re-layouts: 0.95 us -> 0.92 us
where the time goes in v6:
time: 45.5 us; the launch traced here: 45.3 us
  Pallas kernels  42.9 us (94%)
  local copies, waits for them, and re-layouts  1.74 us (4%)
  other arithmetic  0.71 us (2%)
    pallas_call x1, Pallas kernels, on_device(): pl.pallas_call(functools.partial(stack_kernel, ndp, nch, side, mine, laye...  42.9 us
    unnamed x2, local copies, waits for them, and re-layouts  0.92 us

profile of v6, /device:TPU:0, one launch (start us, length us, event | category | flops | bytes accessed | tf_op | source)
XLA Modules:
  0.0 45.3 jit_solution(16330859365645560922)
XLA Ops:
  0.0 0.7 %pad_maximum_fusion.affine = f32[2,6,128]{2,1,0:T(8,128)S(1)} fusion(f32[1,6,128]{2,1,0:T(8,128)} %bitcast.5, f32[1,6,128]{2,1,0:T(8,128)} %bitcast.6), kind=kLoop, calls=%fused_computation | loop fusion | flops 1536 | bytes 12288 | tf_op jit(solution)/shard_map/stack | solution.py:253
  0.7 0.0 copy-start
  0.7 0.9 %copy-done = bf16[2,19,19,128]{3,0,2,1:T(2,128)(2,1)S(1)} copy-done((bf16[2,19,19,128]{3,0,2,1:T(2,128)(2,1)S(1)}, bf16[2,19,19,128]{3,0,2,1:T(2,128)(2,1)}, u32[]{:S(2)}) %copy-start) | copy-done | bytes 184856
  1.6 42.9 %shard_map.46 = bf16[2,19,19,128]{3,2,1,0:T(8,128)(2,1)S(1)} custom-call(bf16[19,19,2,128]{3,2,1,0:T(2,128)(2,1)S(1)} %bitcast.4, bf16[6,2304,128]{2,1,0:T(8,128)(2,1)} %bitcast.7, f32[2,6,128]{2,1,0:T(8,128)S(1)} %pad_maximum_fusion.affine), custom_call_target="tpu_custom_call" | custom-call | flops 2717908992 | bytes 3908608 | tf_op jit(solution)/shard_map/pallas_call | solution.py:223
  44.5 0.8 %copy.5 = bf16[2,19,19,128]{3,0,2,1:T(2,128)(2,1)} copy(bf16[2,19,19,128]{3,2,1,0:T(8,128)(2,1)S(1)} %shard_map.46) | data formatting | bytes 369664 | tf_op jit(solution)/shard_map/pallas_call | solution.py:223
Async XLA Ops:
  0.7 0.9 %copy-start = (bf16[2,19,19,128]{3,0,2,1:T(2,128)(2,1)S(1)}, bf16[2,19,19,128]{3,0,2,1:T(2,128)(2,1)}, u32[]{:S(2)}) copy-start(bf16[2,19,19,128]{3,0,2,1:T(2,128)(2,1)} %param.4) | copy-start | bytes 554500

commit v7 on v6

--- a/solution.py
+++ b/solution.py
@@ -10,7 +10,7 @@
 EPSILON = 1e-05
 MESH = pl.DeviceIdType.MESH
 LANES = 128
-VMEM_LIMIT = 52 * 1024 * 1024
+VMEM_LIMIT = 57 * 1024 * 1024
 
 
 def round_up(value, step):
@@ -19,8 +19,8 @@
 
 def stack_kernel(
     ndp, nch, side, mine, layers, rows, base,
-    boards, weights, affine, out,
-    raw, board_send, board_other, wbuf, aff, xf, skip, mask, lhs, zbuf, stats, stage,
+    boards, weights, gains, shifts, out,
+    raw, board_send, board_other, wbuf, aff, xf, skip, mask, lhs, zbuf, stats, stage, stage_own,
     own_sem, a_local, x_send, x_recv, w_local, w_send, w_recv, s_send, s_recv, o_send, o_recv,
 ):
     dp = lax.axis_index("dp")
@@ -57,8 +57,12 @@
 
     own = pltpu.make_async_copy(boards, raw, own_sem)
     own.start()
-    affine_own = pltpu.make_async_copy(affine, aff.at[me], a_local)
-    affine_own.start()
+    affine_own = [
+        pltpu.make_async_copy(gains, aff.at[me, 0], a_local.at[0]),
+        pltpu.make_async_copy(shifts, aff.at[me, 1], a_local.at[1]),
+    ]
+    for one in affine_own:
+        one.start()
 
     def weight_local(layer):
         return pltpu.make_async_copy(weights.at[layer], wbuf.at[me, layer], w_local.at[layer])
@@ -98,11 +102,13 @@
     pl.semaphore_wait(barrier, total - 1)
     swaps = [
         swap(0, board_send, board_other),
-        swap(1, affine, aff.at[me]),
+        swap(1, gains, aff.at[me, 0]),
+        swap(2, shifts, aff.at[me, 1]),
     ]
     swaps[0].start()
     weight_remote(0, me).start()
     swaps[1].start()
+    swaps[2].start()
 
     def place(half, source):
         for n in range(mine):
@@ -113,26 +119,14 @@
     swaps[0].wait_recv()
     place(other, board_other)
     swaps[1].wait_recv()
-    affine_own.wait()
-
-    def layer_step(layer, carry):
-        odd = lax.rem(layer, 2)
-
-        @pl.when(layer + 1 < layers)
-        def _():
-            weight_remote(layer + 1, me).start()
-
-        for tap in range(9):
-            a, b = divmod(tap, 3)
-            at = base + (a - 1) * stride + (b - 1)
-            for half in range(nch):
-                column = (tap * nch + half) * LANES
-                lhs[:, pl.ds(column, LANES)] = xf[half, pl.ds(at, rows), :].astype(jnp.bfloat16)
-        weight_local(layer).wait()
-        weight_remote(layer, other).wait_recv()
-        kernel = jnp.concatenate([wbuf[half, layer] for half in range(nch)], axis=1)
-        zbuf[...] = jnp.dot(lhs[...], kernel, preferred_element_type=jnp.float32)
-
+    swaps[2].wait_recv()
+    for one in affine_own:
+        one.wait()
+
+    def parity(layer):
+        return layer % 2 if isinstance(layer, int) else lax.rem(layer, 2)
+
+    def send_stats(layer):
         centre = (side // 2) * stride + side // 2
         for half in range(nch):
             lanes = pl.ds(half * LANES, LANES)
@@ -152,14 +146,14 @@
 
         every_peer(send)
 
-        @pl.when(odd == 0)
+        @pl.when(parity(layer) == 0)
         def _():
             for half in range(nch):
                 skip[half] = xf[half, pl.ds(base, rows), :]
 
+    def merged(layer):
         arrived = stats.at[layer, pl.ds(0, total - 1)]
         pltpu.make_async_copy(arrived, arrived, s_recv.at[layer]).wait()
-
         seen = stats[layer]
         mine_mean = stats[layer, flat_me, pl.ds(0, nch), :]
         drift = seen[:, :nch] - mine_mean[None]
@@ -167,18 +161,59 @@
         spread = jnp.sum(points * drift * drift + seen[:, nch:], axis=0)
         mean = mine_mean + shifted * (1.0 / total)
         var = (spread - shifted * shifted * (points / total)) * (1.0 / (points * total))
-        inverse = lax.rsqrt(var + EPSILON)
-        keep = odd.astype(jnp.float32)
+        return mean, lax.rsqrt(var + EPSILON)
+
+    def normalise(layer, half, mean, inverse):
+        keep = 1.0 * parity(layer)
+        gain = aff[half, 0, pl.ds(layer, 1), :] * inverse[half : half + 1]
+        shift = aff[half, 1, pl.ds(layer, 1), :]
+        normed = (zbuf[:, pl.ds(half * LANES, LANES)] - mean[half : half + 1]) * gain + shift
+        normed = normed + skip[half] * keep
+        fresh = jnp.maximum(normed, 0.0) * mask[...]
+        xf[half, pl.ds(base, rows), :] = fresh.astype(jnp.bfloat16).astype(jnp.float32)
+
+    def multiply(layer, half):
+        for tap in range(9):
+            a, b = divmod(tap, 3)
+            at = base + (a - 1) * stride + (b - 1)
+            lhs[half, :, pl.ds(tap * LANES, LANES)] = xf[half, pl.ds(at, rows), :].astype(jnp.bfloat16)
+        kernel = jnp.concatenate([
+            jnp.concatenate([
+                wbuf[column, layer, pl.ds((tap * nch + half) * LANES, LANES), :] for column in range(nch)
+            ], axis=1)
+            for tap in range(9)
+        ], axis=0)
+        return jnp.dot(lhs[half], kernel, preferred_element_type=jnp.float32)
+
+    def weights_ready(layer):
+        weight_local(layer).wait()
+        weight_remote(layer, other).wait_recv()
+
+    if layers > 1:
+        weight_remote(1, me).start()
+    weights_ready(0)
+    zbuf[...] = sum(multiply(0, half) for half in range(nch))
+    send_stats(0)
+
+    def layer_step(layer, carry):
+        @pl.when(layer + 1 < layers)
+        def _():
+            weight_remote(layer + 1, me).start()
+
+        weights_ready(layer)
+        mean, inverse = merged(layer - 1)
+        parts = []
         for half in range(nch):
-            gain = aff[half, 0, pl.ds(layer, 1), :] * inverse[half : half + 1]
-            shift = aff[half, 1, pl.ds(layer, 1), :]
-            normed = (zbuf[:, pl.ds(half * LANES, LANES)] - mean[half : half + 1]) * gain + shift
-            normed = normed + skip[half] * keep
-            fresh = jnp.maximum(normed, 0.0) * mask[...]
-            xf[half, pl.ds(base, rows), :] = fresh.astype(jnp.bfloat16).astype(jnp.float32)
+            normalise(layer - 1, half, mean, inverse)
+            parts.append(multiply(layer, half))
+        zbuf[...] = sum(parts)
+        send_stats(layer)
         return carry
 
-    lax.fori_loop(0, layers, layer_step, 0)
+    lax.fori_loop(1, layers, layer_step, 0)
+    mean, inverse = merged(layers - 1)
+    for half in range(nch):
+        normalise(layers - 1, half, mean, inverse)
 
     def collect(half, target, first):
         for n in range(mine):
@@ -192,7 +227,9 @@
         send_sem=o_send, recv_sem=o_recv, device_id=partner, device_id_type=MESH,
     )
     final.start()
-    collect(me, out, me * mine)
+    collect(me, stage_own, 0)
+    kept = pltpu.make_async_copy(stage_own, out.at[pl.ds(me * mine, mine)], own_sem)
+    kept.start()
 
     for one in swaps:
         one.wait_send()
@@ -204,6 +241,7 @@
         return carry
 
     lax.fori_loop(0, layers, drain, 0)
+    kept.wait()
     final.wait()
 
 
@@ -219,12 +257,11 @@
     depth = 9 * width * nch
     dma = pltpu.SemaphoreType.DMA
     in_hbm = pl.BlockSpec(memory_space=pltpu.HBM)
-    vmem = pl.BlockSpec(memory_space=pltpu.VMEM)
     return pl.pallas_call(
         functools.partial(stack_kernel, ndp, nch, side, mine, layers, rows, base),
         out_shape=jax.ShapeDtypeStruct(boards.shape, jnp.bfloat16),
-        in_specs=[in_hbm] * 3,
-        out_specs=vmem,
+        in_specs=[in_hbm] * 4,
+        out_specs=in_hbm,
         scratch_shapes=[
             pltpu.VMEM((side, side, held, width), jnp.bfloat16),
             pltpu.VMEM((mine, side, side, width), jnp.bfloat16),
@@ -234,11 +271,12 @@
             pltpu.VMEM((nch, span, width), jnp.float32),
             pltpu.VMEM((nch, rows, width), jnp.float32),
             pltpu.VMEM((rows, width), jnp.float32),
-            pltpu.VMEM((rows, depth), jnp.bfloat16),
+            pltpu.VMEM((nch, rows, depth // nch), jnp.bfloat16),
             pltpu.VMEM((rows, width * nch), jnp.float32),
             pltpu.VMEM((layers, total, 2 * nch, width), jnp.float32),
             pltpu.VMEM((mine, side, side, width), jnp.bfloat16),
-            dma, dma, dma((2,)), dma((2,)),
+            pltpu.VMEM((mine, side, side, width), jnp.bfloat16),
+            dma, dma((2,)), dma((3,)), dma((3,)),
             dma((layers,)), dma((layers,)), dma((layers,)),
             dma((layers,)), dma((layers,)), dma, dma,
         ],
@@ -250,7 +288,7 @@
             bytes_accessed=2 * weights.size + 4 * boards.size,
             transcendentals=0,
         ),
-    )(boards.transpose(1, 2, 0, 3), weights.reshape(layers, depth, width), jnp.stack([gains, shifts]))
+    )(boards.transpose(1, 2, 0, 3), weights.reshape(layers, depth, width), gains, shifts)
 
 
 def solution(mesh):

time: 45.5 us -> 44.4 us (0.976)
  other arithmetic: 0.71 us -> 0 us
  Pallas kernels: 42.9 us -> 42.4 us
    pallas_call x1, local copies, waits for them, and re-layouts: 0.82 us -> 1.76 us  [on_device(): pl.pallas_call(functools.partial(stack_kernel, ndp, nch, side, mine, laye...]
    unnamed x2 -> x0, local copies, waits for them, and re-layouts: 0.92 us -> none
    another operation x1 -> x0, other arithmetic: 0.71 us -> none  [on_device(): jnp.stack([gains, shifts])]
where the time goes in v7:
time: 44.4 us; the launch traced here: 44.2 us
  Pallas kernels  42.4 us (95%)
  local copies, waits for them, and re-layouts  1.76 us (4%)
    pallas_call x1, Pallas kernels, on_device(): pl.pallas_call(functools.partial(stack_kernel, ndp, nch, side, mine, laye...  42.4 us
    pallas_call x1, local copies, waits for them, and re-layouts, on_device(): pl.pallas_call(functools.partial(stack_kernel, ndp, nch, side, mine, laye...  1.76 us

profile of v7, /device:TPU:0, one launch (start us, length us, event | category | flops | bytes accessed | tf_op | source)
XLA Modules:
  0.0 44.2 jit_solution(6192103266694503175)
XLA Ops:
  0.0 42.4 %shard_map.46 = bf16[2,19,19,128]{3,2,1,0:T(8,128)(2,1)} custom-call(bf16[19,19,2,128]{3,2,1,0:T(2,128)(2,1)} %bitcast.3, bf16[6,2304,128]{2,1,0:T(8,128)(2,1)} %bitcast.2, f32[6,128]{1,0:T(8,128)} %gains.1, f32[6,128]{1,0:T(8,128)} %shifts.1), custom_call_target="tpu_custom_call" | custom-call | flops 2717908992 | bytes 3908608 | tf_op jit(solution)/shard_map/pallas_call | solution.py:260
  42.4 1.8 %copy.5 = bf16[2,19,19,128]{3,0,2,1:T(2,128)(2,1)} copy(bf16[2,19,19,128]{3,2,1,0:T(8,128)(2,1)} %shard_map.46) | data formatting | bytes 369664 | tf_op jit(solution)/shard_map/pallas_call | solution.py:260

commit v8 on v7

--- a/solution.py
+++ b/solution.py
@@ -172,14 +172,16 @@
         fresh = jnp.maximum(normed, 0.0) * mask[...]
         xf[half, pl.ds(base, rows), :] = fresh.astype(jnp.bfloat16).astype(jnp.float32)
 
-    def multiply(layer, half):
+    def window(half):
         for tap in range(9):
             a, b = divmod(tap, 3)
             at = base + (a - 1) * stride + (b - 1)
             lhs[half, :, pl.ds(tap * LANES, LANES)] = xf[half, pl.ds(at, rows), :].astype(jnp.bfloat16)
+
+    def product(layer, half, columns):
         kernel = jnp.concatenate([
             jnp.concatenate([
-                wbuf[column, layer, pl.ds((tap * nch + half) * LANES, LANES), :] for column in range(nch)
+                wbuf[column, layer, pl.ds((tap * nch + half) * LANES, LANES), :] for column in columns
             ], axis=1)
             for tap in range(9)
         ], axis=0)
@@ -191,8 +193,14 @@
 
     if layers > 1:
         weight_remote(1, me).start()
-    weights_ready(0)
-    zbuf[...] = sum(multiply(0, half) for half in range(nch))
+    for half in range(nch):
+        window(half)
+    weight_local(0).wait()
+    for column in (me, other):
+        if column is other:
+            weight_remote(0, other).wait_recv()
+        lanes = pl.ds(pl.multiple_of(column * LANES, LANES), LANES)
+        zbuf[:, lanes] = sum(product(0, half, [column]) for half in range(nch))
     send_stats(0)
 
     def layer_step(layer, carry):
@@ -205,7 +213,8 @@
         parts = []
         for half in range(nch):
             normalise(layer - 1, half, mean, inverse)
-            parts.append(multiply(layer, half))
+            window(half)
+            parts.append(product(layer, half, range(nch)))
         zbuf[...] = sum(parts)
         send_stats(layer)
         return carry

time: 44.4 us -> 45.2 us (1.018)
  Pallas kernels: 42.4 us -> 43.2 us
    pallas_call x1, Pallas kernels: 42.4 us -> 43.2 us  [on_device(): pl.pallas_call(functools.partial(stack_kernel, ndp, nch, side, mine, laye...]
where the time goes in v8:
time: 45.2 us; the launch traced here: 45 us
  Pallas kernels  43.2 us (96%)
  local copies, waits for them, and re-layouts  1.76 us (4%)
    pallas_call x1, Pallas kernels, on_device(): pl.pallas_call(functools.partial(stack_kernel, ndp, nch, side, mine, laye...  43.2 us
    pallas_call x1, local copies, waits for them, and re-layouts, on_device(): pl.pallas_call(functools.partial(stack_kernel, ndp, nch, side, mine, laye...  1.76 us

profile of v8, /device:TPU:0, one launch (start us, length us, event | category | flops | bytes accessed | tf_op | source)
XLA Modules:
  0.0 45.0 jit_solution(1654840398056056229)
XLA Ops:
  0.0 43.2 %shard_map.46 = bf16[2,19,19,128]{3,2,1,0:T(8,128)(2,1)} custom-call(bf16[19,19,2,128]{3,2,1,0:T(2,128)(2,1)} %bitcast.3, bf16[6,2304,128]{2,1,0:T(8,128)(2,1)} %bitcast.2, f32[6,128]{1,0:T(8,128)} %gains.1, f32[6,128]{1,0:T(8,128)} %shifts.1), custom_call_target="tpu_custom_call" | custom-call | flops 2717908992 | bytes 3908608 | tf_op jit(solution)/shard_map/pallas_call | solution.py:269
  43.2 1.8 %copy.5 = bf16[2,19,19,128]{3,0,2,1:T(2,128)(2,1)} copy(bf16[2,19,19,128]{3,2,1,0:T(8,128)(2,1)} %shard_map.46) | data formatting | bytes 369664 | tf_op jit(solution)/shard_map/pallas_call | solution.py:269

commit v9 on v7

--- a/solution.py
+++ b/solution.py
@@ -20,15 +20,14 @@
 def stack_kernel(
     ndp, nch, side, mine, layers, rows, base,
     boards, weights, gains, shifts, out,
-    raw, board_send, board_other, wbuf, aff, xf, skip, mask, lhs, zbuf, stats, stage, stage_own,
-    own_sem, a_local, x_send, x_recv, w_local, w_send, w_recv, s_send, s_recv, o_send, o_recv,
+    raw, board_send, board_other, wbuf, aff, xf, skip, mask, lhs, zbuf, near, stats, stage, stage_own,
+    own_sem, a_local, x_send, x_recv, w_local, w_send, w_recv, n_send, n_recv, s_send, s_recv, o_send, o_recv,
 ):
     dp = lax.axis_index("dp")
     me = lax.axis_index("chan")
     other = 1 - me
     partner = (dp, other)
     total = ndp * nch
-    flat_me = dp * nch + me
     stride = side + 1
     points = mine * side * side
 
@@ -41,20 +40,19 @@
         return index
 
     def every_peer(body):
-        if total <= 64 and total & (total - 1) == 0:
-            for step in range(total - 1, 0, -1):
-                flat = flip(flat_me, step)
-                body((lax.div(flat, nch), lax.rem(flat, nch)))
+        if ndp <= 32 and ndp & (ndp - 1) == 0:
+            for step in range(ndp - 1, 0, -1):
+                body((flip(dp, step), me))
         else:
             def one(step, carry):
-                flat = lax.rem(flat_me + step, total)
-                body((lax.div(flat, nch), lax.rem(flat, nch)))
+                body((lax.rem(dp + step, ndp), me))
                 return carry
-            lax.fori_loop(1, total, one, 0)
+            lax.fori_loop(1, ndp, one, 0)
 
     barrier = pltpu.get_barrier_semaphore()
     every_peer(lambda peer: pl.semaphore_signal(barrier, inc=1, device_id=peer, device_id_type=MESH))
 
+    pl.semaphore_signal(barrier, inc=1, device_id=partner, device_id_type=MESH)
     own = pltpu.make_async_copy(boards, raw, own_sem)
     own.start()
     affine_own = [
@@ -99,7 +97,7 @@
             xf[me, pl.ds(at, side), :] = kept
             board_send[n, i] = given.astype(jnp.bfloat16)
 
-    pl.semaphore_wait(barrier, total - 1)
+    pl.semaphore_wait(barrier, ndp)
     swaps = [
         swap(0, board_send, board_other),
         swap(1, gains, aff.at[me, 0]),
@@ -126,6 +124,13 @@
     def parity(layer):
         return layer % 2 if isinstance(layer, int) else lax.rem(layer, 2)
 
+    def near_copy(layer):
+        return pltpu.make_async_remote_copy(
+            src_ref=near.at[layer, me], dst_ref=near.at[layer, me],
+            send_sem=n_send.at[layer], recv_sem=n_recv.at[layer],
+            device_id=partner, device_id_type=MESH,
+        )
+
     def send_stats(layer):
         centre = (side // 2) * stride + side // 2
         for half in range(nch):
@@ -134,12 +139,19 @@
             away = (zbuf[:, lanes] - middle) * mask[...]
             first = jnp.sum(away, axis=0, keepdims=True)
             second = jnp.sum(away * away, axis=0, keepdims=True)
-            stats[layer, flat_me, pl.ds(half, 1), :] = middle + first * (1.0 / points)
-            stats[layer, flat_me, pl.ds(nch + half, 1), :] = second - first * first * (1.0 / points)
+            near[layer, me, pl.ds(half, 1), :] = middle + first * (1.0 / points)
+            near[layer, me, pl.ds(nch + half, 1), :] = second - first * first * (1.0 / points)
+
+        near_copy(layer).start()
+        near_copy(layer).wait_recv()
+        pair = [near[layer, core] for core in range(nch)]
+        drift = pair[1][:nch] - pair[0][:nch]
+        stats[layer, dp, pl.ds(0, nch), :] = pair[0][:nch] + 0.5 * drift
+        stats[layer, dp, pl.ds(nch, nch), :] = pair[0][nch:] + pair[1][nch:] + (0.5 * points) * drift * drift
 
         def send(peer):
             pltpu.make_async_remote_copy(
-                src_ref=stats.at[layer, flat_me], dst_ref=stats.at[layer, flat_me],
+                src_ref=stats.at[layer, dp], dst_ref=stats.at[layer, dp],
                 send_sem=s_send.at[layer], recv_sem=s_recv.at[layer],
                 device_id=peer, device_id_type=MESH,
             ).start()
@@ -152,15 +164,15 @@
                 skip[half] = xf[half, pl.ds(base, rows), :]
 
     def merged(layer):
-        arrived = stats.at[layer, pl.ds(0, total - 1)]
+        arrived = stats.at[layer, pl.ds(0, ndp - 1)]
         pltpu.make_async_copy(arrived, arrived, s_recv.at[layer]).wait()
         seen = stats[layer]
-        mine_mean = stats[layer, flat_me, pl.ds(0, nch), :]
+        mine_mean = stats[layer, dp, pl.ds(0, nch), :]
         drift = seen[:, :nch] - mine_mean[None]
         shifted = jnp.sum(drift, axis=0)
-        spread = jnp.sum(points * drift * drift + seen[:, nch:], axis=0)
-        mean = mine_mean + shifted * (1.0 / total)
-        var = (spread - shifted * shifted * (points / total)) * (1.0 / (points * total))
+        spread = jnp.sum(points * nch * drift * drift + seen[:, nch:], axis=0)
+        mean = mine_mean + shifted * (1.0 / ndp)
+        var = (spread - shifted * shifted * (points * nch / ndp)) * (1.0 / (points * total))
         return mean, lax.rsqrt(var + EPSILON)
 
     def normalise(layer, half, mean, inverse):
@@ -236,7 +248,8 @@
 
     def drain(layer, carry):
         weight_remote(layer, me).wait_send()
-        sent = stats.at[layer, pl.ds(0, total - 1)]
+        near_copy(layer).wait_send()
+        sent = stats.at[layer, pl.ds(0, ndp - 1)]
         pltpu.make_async_copy(sent, sent, s_send.at[layer]).wait()
         return carry
 
@@ -273,12 +286,13 @@
             pltpu.VMEM((rows, width), jnp.float32),
             pltpu.VMEM((nch, rows, depth // nch), jnp.bfloat16),
             pltpu.VMEM((rows, width * nch), jnp.float32),
-            pltpu.VMEM((layers, total, 2 * nch, width), jnp.float32),
+            pltpu.VMEM((layers, nch, 2 * nch, width), jnp.float32),
+            pltpu.VMEM((layers, ndp, 2 * nch, width), jnp.float32),
             pltpu.VMEM((mine, side, side, width), jnp.bfloat16),
             pltpu.VMEM((mine, side, side, width), jnp.bfloat16),
             dma, dma((2,)), dma((3,)), dma((3,)),
             dma((layers,)), dma((layers,)), dma((layers,)),
-            dma((layers,)), dma((layers,)), dma, dma,
+            dma((layers,)), dma((layers,)), dma((layers,)), dma((layers,)), dma, dma,
         ],
         compiler_params=pltpu.CompilerParams(
             collective_id=0, has_side_effects=True, vmem_limit_bytes=VMEM_LIMIT

time: 44.4 us -> 47.3 us (1.065)
  Pallas kernels: 42.4 us -> 45.4 us
    pallas_call x1, Pallas kernels: 42.4 us -> 45.4 us  [on_device(): pl.pallas_call(functools.partial(stack_kernel, ndp, nch, side, mine, laye...]
where the time goes in v9:
time: 47.3 us; the launch traced here: 47.2 us
  Pallas kernels  45.4 us (96%)
  local copies, waits for them, and re-layouts  1.76 us (4%)
    pallas_call x1, Pallas kernels, on_device(): pl.pallas_call(functools.partial(stack_kernel, ndp, nch, side, mine, laye...  45.4 us
    pallas_call x1, local copies, waits for them, and re-layouts, on_device(): pl.pallas_call(functools.partial(stack_kernel, ndp, nch, side, mine, laye...  1.76 us

profile of v9, /device:TPU:0, one launch (start us, length us, event | category | flops | bytes accessed | tf_op | source)
XLA Modules:
  0.0 47.2 jit_solution(5521873176300614065)
XLA Ops:
  0.0 45.4 %shard_map.46 = bf16[2,19,19,128]{3,2,1,0:T(8,128)(2,1)} custom-call(bf16[19,19,2,128]{3,2,1,0:T(2,128)(2,1)} %bitcast.3, bf16[6,2304,128]{2,1,0:T(8,128)(2,1)} %bitcast.2, f32[6,128]{1,0:T(8,128)} %gains.1, f32[6,128]{1,0:T(8,128)} %shifts.1), custom_call_target="tpu_custom_call" | custom-call | flops 2717908992 | bytes 3908608 | tf_op jit(solution)/shard_map/pallas_call | solution.py:273
  45.4 1.8 %copy.5 = bf16[2,19,19,128]{3,0,2,1:T(2,128)(2,1)} copy(bf16[2,19,19,128]{3,2,1,0:T(8,128)(2,1)} %shard_map.46) | data formatting | bytes 369664 | tf_op jit(solution)/shard_map/pallas_call | solution.py:273
